TPU v7x, 32 devices: a whole 2x2x4 slice. The times are simulated.
32 devices in a mesh: dom: 2 (over x), tensor: 16 (over z, y, core).
Axes of the slice: x: 2, y: 2, z: 4, core: 2. Of those that a mesh axis runs over, the one named last changes fastest.
Arguments:
- attn_input: bfloat16 [8, 512, 8192], P('dom', None, 'tensor'), parts along dimension 0, may hold values from -6 to 6
- grad_query: bfloat16 [8, 512, 8192], P('dom', None, 'tensor'), parts along dimension 0, may hold values from -24 to 24
- grad_key_value: bfloat16 [8, 512, 2, 1024], P('dom', None, None, 'tensor'), parts along dimension 0, may hold values from -24 to 24
- attn_mixed: bfloat16 [8, 512, 8192], P('dom', None, 'tensor'), parts along dimension 0, may hold values from -6 to 6
- grad_attn_out: bfloat16 [8, 512, 8192], P('dom', None, 'tensor'), parts along dimension 0, may hold values from -24 to 24
- mlp_input: bfloat16 [8, 512, 8192], P('dom', None, 'tensor'), parts along dimension 0, may hold values from -6 to 6
- grad_gate_up: bfloat16 [8, 512, 2, 28672], P('dom', None, None, 'tensor'), parts along dimension 0, may hold values from -24 to 24
- hidden_acts: bfloat16 [8, 512, 28672], P('dom', None, 'tensor'), parts along dimension 0, may hold values from -6 to 6
- grad_mlp_out: bfloat16 [8, 512, 8192], P('dom', None, 'tensor'), parts along dimension 0, may hold values from -24 to 24
- in_attn: bfloat16 [3, 8192, 64], P(None, 'tensor'), may hold values from -0.0625 to 0.0625
- in_mixed: bfloat16 [8192, 64], P('tensor'), may hold values from -0.0625 to 0.0625
- in_mlp: bfloat16 [2, 8192, 64], P(None, 'tensor'), may hold values from -0.0625 to 0.0625
- in_hidden: bfloat16 [28672, 64], P('tensor'), may hold values from -0.03125 to 0.03125
- out_query: bfloat16 [8192, 64], P('tensor'), may hold values from -0.0625 to 0.0625
- out_key_value: bfloat16 [2, 1024, 64], P(None, 'tensor'), may hold values from -0.1875 to 0.1875
- out_attn: bfloat16 [8192, 64], P('tensor'), may hold values from -0.0625 to 0.0625
- out_gate_up: bfloat16 [2, 28672, 64], P(None, 'tensor'), may hold values from -0.03125 to 0.03125
- out_mlp: bfloat16 [8192, 64], P('tensor'), may hold values from -0.0625 to 0.0625
- queries: bfloat16 [256, 28672], P(None, 'tensor'), may hold values from -0.125 to 0.125
- lengths: int32 [8], P('dom'), parts along dimension 0, may hold values from 1 to 512, 1024 in all
Outputs:
- train_grads: bfloat16 [8, 28672], P('dom', 'tensor'), parts along dimension 0
- scores: float32 [8, 256], P('dom', 'tensor'), parts along dimension 0
There are 2 independent parts, one for each index of `dom`. A program takes and returns all parts, laid end to end along the dimension named above; an argument that names none is the same for every part. Nothing has to cross between parts.
Inputs may be any that keep to these rules, and one draw needn't show every extreme that they name: The lengths of one job sum to 1024, and the largest is 512.
All inputs are finite; a program needn't handle non-finite values.
Results may differ from a plain program's by a relative error of at most 0.0032.
Values sent between devices are 32-bit elements; how exact they have to be, the bound alone decides.
A program may use at most 192 MiB of HBM per device.

v0:
```python
import jax
import jax.numpy as jnp
from jax import lax
from jax.sharding import PartitionSpec as P


def project_pair(inputs, factor_in, gradients, factor_out):
    row_total = inputs.shape[0] * inputs.shape[1]
    in_proj = jnp.dot(inputs.reshape(row_total, -1), factor_in, preferred_element_type=jnp.float32)
    out_proj = jnp.dot(
        gradients.reshape(row_total, -1), factor_out, preferred_element_type=jnp.float32
    )
    return jnp.concatenate([in_proj, out_proj], axis=1)


def body(
    attn_input,
    grad_query,
    grad_key_value,
    attn_mixed,
    grad_attn_out,
    mlp_input,
    grad_gate_up,
    hidden_acts,
    grad_mlp_out,
    in_attn,
    in_mixed,
    in_mlp,
    in_hidden,
    out_query,
    out_key_value,
    out_attn,
    out_gate_up,
    out_mlp,
    queries,
    lengths,
):
    seq_count = attn_input.shape[0]
    maxlen = attn_input.shape[1]
    proj_rank = in_mixed.shape[1]
    seq_index = jnp.arange(seq_count, dtype=jnp.int32)
    pieces = [
        project_pair(attn_input, in_attn[0], grad_query, out_query),
        project_pair(attn_input, in_attn[1], grad_key_value[:, :, 0], out_key_value[0]),
        project_pair(attn_input, in_attn[2], grad_key_value[:, :, 1], out_key_value[1]),
        project_pair(attn_mixed, in_mixed, grad_attn_out, out_attn),
        project_pair(mlp_input, in_mlp[0], grad_gate_up[:, :, 0], out_gate_up[0]),
        project_pair(mlp_input, in_mlp[1], grad_gate_up[:, :, 1], out_gate_up[1]),
        project_pair(hidden_acts, in_hidden, grad_mlp_out, out_mlp),
    ]
    joined = jnp.concatenate(pieces, axis=1)
    summed = lax.psum_scatter(joined, "tensor", scatter_dimension=0, tiled=True)
    received = summed.reshape(summed.shape[0], 7, 2 * proj_rank)
    row_count = received.shape[0]
    global_ids = lax.axis_index("tensor") * row_count + jnp.arange(row_count, dtype=jnp.int32)
    owner_seq = global_ids // maxlen
    offset = global_ids - owner_seq * maxlen
    matches = owner_seq[:, None] == seq_index[None, :]
    seq_len = jnp.sum(jnp.where(matches, lengths[None, :], 0), axis=1)
    weight = (matches & (offset < seq_len)[:, None]).astype(jnp.float32)
    weight = weight / lengths.astype(jnp.float32)[None, :]
    in_proj = received[:, :, :proj_rank]
    out_proj = received[:, :, proj_rank:]
    partial_value = jnp.einsum(
        "rs,rmi,rmj->smij", weight, in_proj, out_proj, precision=lax.Precision.HIGHEST
    )
    partial_value = partial_value.reshape(seq_count, -1)
    grad_shard = lax.psum_scatter(partial_value, "tensor", scatter_dimension=1, tiled=True)
    train_grads = grad_shard.astype(jnp.bfloat16)
    partial_scores = lax.dot_general(
        train_grads, queries, (((1,), (1,)), ((), ())), preferred_element_type=jnp.float32
    )
    scores = lax.psum_scatter(partial_scores, "tensor", scatter_dimension=1, tiled=True)
    return (train_grads, scores)


def solution(mesh):
    return jax.shard_map(
        body,
        mesh=mesh,
        in_specs=(
            P("dom", None, "tensor"),
            P("dom", None, "tensor"),
            P("dom", None, None, "tensor"),
            P("dom", None, "tensor"),
            P("dom", None, "tensor"),
            P("dom", None, "tensor"),
            P("dom", None, None, "tensor"),
            P("dom", None, "tensor"),
            P("dom", None, "tensor"),
            P(None, "tensor", None),
            P("tensor", None),
            P(None, "tensor", None),
            P("tensor", None),
            P("tensor", None),
            P(None, "tensor", None),
            P("tensor", None),
            P(None, "tensor", None),
            P("tensor", None),
            P(None, "tensor"),
            P("dom"),
        ),
        out_specs=(P("dom", "tensor"), P("dom", "tensor")),
        check_vma=False,
    )
```

profile of v0, /device:TPU:0, one launch (start us, length us, event | category | flops | bytes accessed | tf_op | source)
XLA Modules:
  0.0 413.9 jit_solution(10603037511576203435)
XLA Ops:
  7.2 0.0 copy-start
  7.2 0.0 reduce-scatter.8.cloned.1.call-start
  7.2 1.5 copy-done
  8.8 2.6 convolution_dynamic-update-slice_fusion.13
  11.3 3.9 convolution_dynamic-update-slice_fusion.12
  15.2 2.4 convolution_dynamic-update-slice_fusion.11
  17.6 1.1 fusion.23
  18.7 0.2 copy.27
  18.9 1.8 convolution_dynamic-update-slice_fusion.10
  20.8 2.4 convolution_dynamic-update-slice_fusion.9
  23.2 0.2 copy.28
  23.4 0.0 copy-done.2
  23.4 22.2 %fusion.22 = (bf16[4,512,1,1792]{3,2,1,0:T(2,128)(2,1)}, bf16[4,512,1,1792]{3,2,1,0:T(2,128)(2,1)}) fusion(bf16[4,512,2,1792]{3,2,1,0:T(2,128)(2,1)S(1)} %copy-done.2), kind=kLoop, calls=%fused_computation.48 | loop fusion | bytes 29360128 | tf_op jit(solution)/shard_map/slice | solution.py:48
  45.7 0.0 copy-start.9
  45.7 0.0 copy-start.10
  45.7 0.0 copy-start.4
  45.7 0.0 copy-start.8
  45.7 9.5 %copy.39 = bf16[4,512,1,1792]{3,1,0,2:T(8,128)(2,1)} copy(bf16[4,512,1,1792]{3,2,1,0:T(2,128)(2,1)} %get-tuple-element.3) | data formatting | bytes 14680064
  55.3 0.0 copy-done.12
  55.3 1.1 convolution_dynamic-update-slice_fusion.8
  56.3 3.8 convolution_dynamic-update-slice_fusion.7
  60.1 3.1 convolution_dynamic-update-slice_fusion.6
  63.3 0.0 copy-done.8
  63.3 1.6 convolution_dynamic-update-slice_fusion.5
  64.8 0.0 copy-done.3
  64.8 3.1 convolution_dynamic-update-slice_fusion.4
  68.0 1.5 convolution_dynamic-update-slice_fusion.3
  69.5 9.4 %copy.40 = bf16[4,512,1,1792]{3,1,0,2:T(8,128)(2,1)} copy(bf16[4,512,1,1792]{3,2,1,0:T(2,128)(2,1)} %get-tuple-element.2) | data formatting | bytes 14680064
  78.9 6.3 %convolution_dynamic-update-slice_fusion.2 = f32[2048,896]{0,1:T(8,128)} fusion(f32[2048,896]{0,1:T(8,128)} %convolution_dynamic-update-slice_fusion.3, bf16[2048,1792]{1,0:T(8,128)(2,1)} %bitcast.87, bf16[2,1792,64]{1,2,0:T(8,128)(2,1)S(1)} %copy-done.6), kind=kOutput, calls=%fused_computation.2 | convolution fusion | flops 469762048 | bytes 8093696 | tf_op jit(solution)/shard_map/dot_general | solution.py:10
  85.2 6.2 %convolution_dynamic-update-slice_fusion.1 = f32[2048,896]{0,1:T(8,128)} fusion(f32[2048,896]{0,1:T(8,128)} %convolution_dynamic-update-slice_fusion.2, bf16[2048,1792]{1,0:T(8,128)(2,1)} %bitcast.90, bf16[1792,64]{0,1:T(8,128)(2,1)S(1)} %copy-done.7), kind=kOutput, calls=%fused_computation.1 | convolution fusion | flops 469762048 | bytes 8093696 | tf_op jit(solution)/shard_map/dot_general | solution.py:9
  91.5 0.0 copy-done.5
  91.5 1.6 convolution_dynamic-update-slice_fusion
  93.1 0.0 reduce-scatter.8.cloned.1.call-update
  93.1 0.0 reduce-scatter.10.cloned.1.call-start
  93.2 0.1 select_reduce_fusion
  93.3 0.1 convert_divide_fusion
  93.4 94.3 %reduce-scatter.8.cloned.1.call-done = f32[128,896]{0,1:T(8,128)} async-done(((f32[2048,896]{0,1:T(8,128)}), f32[128,896]{0,1:T(8,128)}) %reduce-scatter.8.cloned.1.call-update) | async-done | bytes 458768 | tf_op jit(solution)/shard_map/reduce_scatter | solution.py:52
  187.7 1.0 slice.60
  188.6 1.9 convolution_bitcast_fusion
  190.5 8.3 %copy.37 = f32[4,7,64,64]{0,3,2,1:T(8,128)} copy(f32[4,7,64,64]{3,2,0,1:T(8,128)S(1)} %convolution_bitcast_fusion) | data formatting | bytes 917504
  198.8 0.0 reduce-scatter.10.cloned.1.call-update
  198.8 0.0 reduce-scatter.12.cloned.1.call-start
  198.9 149.4 %reduce-scatter.10.cloned.1.call-done = f32[1792,4]{1,0:T(8,128)} async-done(((f32[28672,4]{1,0:T(8,128)}), f32[1792,4]{1,0:T(8,128)}) %reduce-scatter.10.cloned.1.call-update) | async-done | bytes 28688
  348.3 1.5 copy.34
  349.8 1.0 convolution_bitcast_fusion.1
  350.8 0.0 reduce-scatter.12.cloned.1.call-update
  350.8 55.1 %reduce-scatter.12.cloned.1.call-done = f32[16,4]{1,0:T(8,128)} async-done(((f32[256,4]{1,0:T(8,128)}), f32[16,4]{1,0:T(8,128)}) %reduce-scatter.12.cloned.1.call-update) | async-done | bytes 272
  406.0 1.3 copy.36
  (26 shorter events, 0.2 us)
Async XLA Ops:
  7.2 1.6 copy-start
  7.2 180.5 %reduce-scatter.8.cloned.1.call-start = ((), (), s32[]{:S(2)}) async-start(), calls=%async_computation.3 | async-start | bytes 7798784 | tf_op jit(solution)/shard_map/reduce_scatter | solution.py:52
  8.8 14.7 %copy-start.2 = (bf16[4,512,2,1792]{3,2,1,0:T(2,128)(2,1)S(1)}, bf16[4,512,2,1792]{3,2,1,0:T(2,128)(2,1)}, u32[]{:S(2)}) copy-start(bf16[4,512,2,1792]{3,2,1,0:T(2,128)(2,1)} %param.26) | copy-start | bytes 44040196
  45.7 9.6 %copy-start.12 = (bf16[2,64,64]{2,1,0:T(8,128)(2,1)S(1)}, bf16[2,64,64]{2,1,0:T(8,128)(2,1)}, u32[]{:S(2)}) copy-start(bf16[2,64,64]{2,1,0:T(8,128)(2,1)} %param.34) | copy-start | bytes 49156
  45.7 10.7 %copy-start.9 = (bf16[512,64]{0,1:T(8,128)(2,1)S(1)}, bf16[512,64]{0,1:T(8,128)(2,1)}, u32[]{:S(2)}) copy-start(bf16[512,64]{0,1:T(8,128)(2,1)} %param.30) | copy-start | bytes 196612
  45.7 14.5 %copy-start.10 = (bf16[512,64]{0,1:T(8,128)(2,1)S(1)}, bf16[512,64]{0,1:T(8,128)(2,1)}, u32[]{:S(2)}) copy-start(bf16[512,64]{0,1:T(8,128)(2,1)} %param.35) | copy-start | bytes 196612
  45.7 17.6 %copy-start.4 = (bf16[4,512,512]{2,1,0:T(8,128)(2,1)S(1)}, bf16[4,512,512]{2,1,0:T(8,128)(2,1)}, u32[]{:S(2)}) copy-start(bf16[4,512,512]{2,1,0:T(8,128)(2,1)} %param.25) | copy-start | bytes 6291460
  45.7 17.6 %copy-start.8 = (bf16[2,512,64]{1,2,0:T(8,128)(2,1)S(1)}, bf16[2,512,64]{1,2,0:T(8,128)(2,1)}, u32[]{:S(2)}) copy-start(bf16[2,512,64]{1,2,0:T(8,128)(2,1)} %param.31) | copy-start | bytes 393220
  55.3 9.6 %copy-start.3 = (bf16[4,512,1,1792]{3,1,0,2:T(8,128)(2,1)S(1)}, bf16[4,512,1,1792]{3,1,0,2:T(8,128)(2,1)}, u32[]{:S(2)}) copy-start(bf16[4,512,1,1792]{3,1,0,2:T(8,128)(2,1)} %copy.39) | copy-start | bytes 22020100
  55.3 9.6 %copy-start.6 = (bf16[2,1792,64]{1,2,0:T(8,128)(2,1)S(1)}, bf16[2,1792,64]{1,2,0:T(8,128)(2,1)}, u32[]{:S(2)}) copy-start(bf16[2,1792,64]{1,2,0:T(8,128)(2,1)} %param.36) | copy-start | bytes 1376260
  78.9 6.4 %copy-start.7 = (bf16[1792,64]{0,1:T(8,128)(2,1)S(1)}, bf16[1792,64]{0,1:T(8,128)(2,1)}, u32[]{:S(2)}) copy-start(bf16[1792,64]{0,1:T(8,128)(2,1)} %param.32) | copy-start | bytes 688132
  78.9 12.6 %copy-start.5 = (bf16[4,512,512]{2,1,0:T(8,128)(2,1)S(1)}, bf16[4,512,512]{2,1,0:T(8,128)(2,1)}, u32[]{:S(2)}) copy-start(bf16[4,512,512]{2,1,0:T(8,128)(2,1)} %param.28) | copy-start | bytes 6291460
  78.9 12.6 %copy-start.11 = (bf16[512,64]{0,1:T(8,128)(2,1)S(1)}, bf16[512,64]{0,1:T(8,128)(2,1)}, u32[]{:S(2)}) copy-start(bf16[512,64]{0,1:T(8,128)(2,1)} %param.37) | copy-start | bytes 196612
  85.2 7.9 %copy-start.15 = (s32[4]{0:T(128)S(1)}, s32[4]{0:T(128)}, u32[]{:S(2)}) copy-start(s32[4]{0:T(128)} %param.39) | copy-start | bytes 52
  93.1 255.2 %reduce-scatter.10.cloned.1.call-start = ((), (), s32[]{:S(2)}) async-start(), calls=%async_computation.4 | async-start | bytes 15597568
  198.8 208.5 %copy-start.1 = (bf16[4,512,512]{2,1,0:T(8,128)(2,1)S(1)}, bf16[4,512,512]{2,1,0:T(8,128)(2,1)}, u32[]{:S(2)}) copy-start(bf16[4,512,512]{2,1,0:T(8,128)(2,1)} %param.20) | copy-start | bytes 6291460
  198.8 151.0 %copy-start.14 = (bf16[256,1792]{1,0:T(8,128)(2,1)S(1)}, bf16[256,1792]{1,0:T(8,128)(2,1)}, u32[]{:S(2)}) copy-start(bf16[256,1792]{1,0:T(8,128)(2,1)} %param.38) | copy-start | bytes 2752516
  198.8 207.1 %reduce-scatter.12.cloned.1.call-start = ((), (), s32[]{:S(2)}) async-start(), calls=%async_computation.5 | async-start | bytes 139264
  349.8 57.5 %copy-start.13 = (bf16[4,1792]{1,0:T(4,128)(2,1)}, bf16[4,1792]{1,0:T(4,128)(2,1)S(1)}, u32[]{:S(2)}) copy-start(bf16[4,1792]{1,0:T(4,128)(2,1)S(1)} %copy.34) | copy-start | bytes 43012
Sparse Core Ops, SparseCore 0:
  93.2 94.4 reduce-scatter.7
  199.0 149.2 reduce-scatter.9
  351.8 54.1 reduce-scatter.11
where the time goes:
time: 414 us
  waiting for transfers between devices  299 us (72%)
  local copies, waits for them, and re-layouts  56.4 us (14%)
  matrix products  44.3 us (11%)
  between operations  13.9 us (3%)
    unnamed x5, waiting for transfers between devices  205 us
    reduce_scatter x1, waiting for transfers between devices, body(): summed = lax.psum_scatter(joined, 'tensor', scatter_dimension=0, tiled=True)  94.3 us
    unnamed x39, local copies, waits for them, and re-layouts  31.8 us
    slice x1, local copies, waits for them, and re-layouts, body(): grad_gate_up[:, :, 1]  22.2 us
    dot_general x7, matrix products, project_pair(): jnp.dot(gradients.reshape(row_total, -1), factor_out, preferred_element_t...  21 us
    dot_general x7, matrix products, project_pair(): jnp.dot(inputs.reshape(row_total, -1), factor_in, preferred_element_type=...  20.5 us
  transfers between devices with their start and end apart: 3, of which 3 were waited for; matrix products, arithmetic and copies ran while one was open for 0% of the time, Pallas kernels for 0%

commit v1 on v0

v1 whole, which is shorter than its diff:
```python
import functools
import jax
import jax.numpy as jnp
from jax import lax
from jax.experimental import pallas as pl
from jax.experimental.pallas import tpu as pltpu
from jax.sharding import PartitionSpec as P

BLOCK = 128
MODULES = 7
MESH = pl.DeviceIdType.MESH
NT = (((1,), (1,)), ((), ()))
TN = (((0,), (0,)), ((), ()))


def mm(a, b, dims=NT):
    return lax.dot_general(a, b, dims, preferred_element_type=jnp.float32)


def project_kernel(
    live_rows,
    table,
    attn_input,
    grad_query,
    grad_kv,
    attn_mixed,
    grad_attn,
    mlp_input,
    grad_gate_up,
    hidden,
    grad_mlp,
    in_attn,
    in_mixed,
    in_mlp,
    in_hidden,
    out_query,
    out_kv,
    out_attn,
    out_gate_up,
    out_mlp,
    out,
    w_attn,
    w_mlp,
    w_mixed,
    w_hidden,
    w_query,
    w_oattn,
    w_omlp,
    w_gu,
    w_kv,
    mixed_rows,
    rows,
    sem,
):
    i = pl.program_id(0)
    r = in_mixed.shape[0]

    @pl.when(i == 0)
    def _():
        for ref in (w_attn, w_mlp, w_mixed, w_hidden, w_query, w_oattn, w_omlp, w_gu, w_kv):
            ref[...] = jnp.zeros_like(ref)
        for m in range(3):
            w_attn[2 * r * m : 2 * r * m + r, :] = in_attn[m]
        for m in range(2):
            w_mlp[2 * r * m : 2 * r * m + r, :] = in_mlp[m]
            w_gu[2 * r * m + r : 2 * r * m + 2 * r, :] = out_gate_up[m]
            w_kv[m, :, r : 2 * r] = out_kv[m]
        w_mixed[:r, :] = in_mixed[...]
        w_hidden[:r, :] = in_hidden[...]
        w_query[r : 2 * r, :] = out_query[...]
        w_oattn[r : 2 * r, :] = out_attn[...]
        w_omlp[r : 2 * r, :] = out_mlp[...]

    @pl.when(table[3, i] > 0)
    def _():
        start = table[2, i]

        def put(m, value):
            rows[m, pl.ds(start, BLOCK), :] = value

        both = grad_gate_up[0].reshape(2 * BLOCK, grad_gate_up.shape[-1])
        rows_gu = mm(both, w_gu[...])
        mixed_rows[0] = rows_gu[:, : 2 * r]
        mixed_rows[1] = rows_gu[:, 2 * r :]
        first = mm(attn_input[0], w_attn[...])
        put(0, first[:, : 2 * r] + mm(grad_query[0], w_query[...]))
        put(1, first[:, 2 * r : 4 * r] + mm(grad_kv[0, 0], w_kv[0], TN))
        put(2, first[:, 4 * r :] + mm(grad_kv[0, 1], w_kv[1], TN))
        put(3, mm(attn_mixed[0], w_mixed[...]) + mm(grad_attn[0], w_oattn[...]))
        second = mm(mlp_input[0], w_mlp[...])
        put(4, second[:, : 2 * r] + mixed_rows[0, pl.ds(0, BLOCK, stride=2), :])
        put(5, second[:, 2 * r :] + mixed_rows[1, pl.ds(1, BLOCK, stride=2), :])
        put(6, mm(hidden[0], w_hidden[...]) + mm(grad_mlp[0], w_omlp[...]))

    @pl.when(i == pl.num_programs(0) - 1)
    def _():
        copy = pltpu.make_async_copy(rows.at[:, pl.ds(0, live_rows), :], out, sem)
        copy.start()
        copy.wait()


def project(arrays, lengths, live_rows):
    (
        attn_input, grad_query, grad_kv, attn_mixed, grad_attn, mlp_input, grad_gate_up, hidden, grad_mlp,
        in_attn, in_mixed, in_mlp, in_hidden, out_query, out_kv, out_attn, out_gate_up, out_mlp,
    ) = arrays
    seqs, maxlen = attn_input.shape[:2]
    r = in_mixed.shape[1]
    steps = maxlen // BLOCK + (live_rows - maxlen + (seqs - 1) * (BLOCK - 1)) // BLOCK
    counts = (lengths + BLOCK - 1) // BLOCK
    ends = jnp.cumsum(counts)
    starts = jnp.cumsum(lengths) - lengths
    ids = jnp.arange(steps, dtype=jnp.int32)
    at = jnp.minimum(ids, ends[-1] - 1)
    seq = jnp.sum((at[:, None] >= ends[None, :]).astype(jnp.int32), axis=1)
    pick = seq[:, None] == jnp.arange(seqs, dtype=jnp.int32)[None, :]
    first = jnp.sum(jnp.where(pick, (ends - counts)[None, :], 0), axis=1)
    begin = jnp.sum(jnp.where(pick, starts[None, :], 0), axis=1)
    block = at - first
    table = jnp.stack([seq, block, begin + block * BLOCK, (ids < ends[-1]).astype(jnp.int32)])

    grad_kv = jnp.transpose(grad_kv, (0, 2, 3, 1))
    tr = lambda x: jnp.swapaxes(x, -1, -2)
    factors = [
        tr(in_attn), tr(in_mixed), tr(in_mlp), tr(in_hidden), tr(out_query), out_kv, tr(out_attn),
        tr(out_gate_up), tr(out_mlp),
    ]
    data = [attn_input, grad_query, grad_kv, attn_mixed, grad_attn, mlp_input, grad_gate_up, hidden, grad_mlp]

    def spec(x):
        if x is grad_kv:
            return pl.BlockSpec((1,) + x.shape[1:3] + (BLOCK,), lambda i, t: (t[0, i], 0, 0, t[1, i]))
        rest = x.shape[2:]
        return pl.BlockSpec((1, BLOCK) + rest, lambda i, t: (t[0, i], t[1, i]) + (0,) * len(rest))

    def whole(x):
        return pl.BlockSpec(x.shape, lambda i, t: (0,) * x.ndim)

    bf = jnp.bfloat16
    width = attn_input.shape[2]
    ff = hidden.shape[2]
    return pl.pallas_call(
        functools.partial(project_kernel, live_rows),
        grid_spec=pltpu.PrefetchScalarGridSpec(
            num_scalar_prefetch=1,
            grid=(steps,),
            in_specs=[spec(x) for x in data] + [whole(x) for x in factors],
            out_specs=pl.BlockSpec(memory_space=pl.ANY),
            scratch_shapes=[
                pltpu.VMEM((6 * r, width), bf),
                pltpu.VMEM((4 * r, width), bf),
                pltpu.VMEM((2 * r, width), bf),
                pltpu.VMEM((2 * r, ff), bf),
                pltpu.VMEM((2 * r, width), bf),
                pltpu.VMEM((2 * r, width), bf),
                pltpu.VMEM((2 * r, width), bf),
                pltpu.VMEM((4 * r, ff), bf),
                pltpu.VMEM((2, grad_kv.shape[2], 2 * r), bf),
                pltpu.VMEM((2, 2 * BLOCK, 2 * r), jnp.float32),
                pltpu.VMEM((MODULES, live_rows + BLOCK, 2 * r), jnp.float32),
                pltpu.SemaphoreType.DMA,
            ],
        ),
        out_shape=jax.ShapeDtypeStruct((MODULES, live_rows, 2 * r), jnp.float32),
        compiler_params=pltpu.CompilerParams(vmem_limit_bytes=60 * 2**20),
    )(table, *data, *factors)


def reduce_kernel(n, bits, q_own, seqs, proj, weight, queries, grads_out, scores_out, *scratch):
    kept = scratch[0]
    bufs = scratch[1 : 1 + bits]
    send2 = scratch[1 + bits]
    bufs2 = scratch[2 + bits : 2 + 2 * bits]
    score = scratch[2 + 2 * bits]
    score_in = scratch[3 + 2 * bits]
    kept_sem, s1, r1, s2, r2, s3, r3 = scratch[4 + 2 * bits :]
    me = lax.axis_index("tensor")
    mine = [lax.rem(me // (1 << j), 2) for j in range(bits)]
    partner = [me + (1 - 2 * mine[j]) * (1 << j) for j in range(bits)]
    r = proj.shape[-1] // 2

    barrier = pltpu.get_barrier_semaphore()
    for j in range(bits):
        pl.semaphore_signal(barrier, inc=1, device_id={"tensor": partner[j]}, device_id_type=MESH)
    pl.semaphore_wait(barrier, bits)

    def part(ref, lead, j, which):
        return ref.at[lead + (slice(None),) * (bits - 1 - j) + (which,)]

    def send(ref, lead, into, into_lead, j, ss, rs):
        return pltpu.make_async_remote_copy(
            src_ref=part(ref, lead, j, 1 - mine[j]),
            dst_ref=into.at[into_lead] if into_lead else into,
            send_sem=ss,
            recv_sem=rs,
            device_id={"tensor": partner[j]},
            device_id_type=MESH,
        )

    def copy1(m, j):
        source = proj if j == 0 else bufs[j - 1]
        return send(source, (m,), bufs[j], (m,), j, s1.at[m, j], r1.at[m, j])

    def keep(m):
        return pltpu.make_async_copy(part(proj, (m,), 0, mine[0]), kept.at[m], kept_sem.at[m])

    for m in range(MODULES):
        copy1(m, 0).start()
        keep(m).start()

    def take(m, j):
        copy1(m, j).wait()
        if j == 0:
            keep(m).wait()
            bufs[0][m] = bufs[0][m] + kept[m]
        else:
            bufs[j][m] = bufs[j][m] + part(bufs[j - 1], (m,), j, mine[j])[...]
        if j + 1 < bits:
            copy1(m, j + 1).start()

    rows_own = send2.shape[-2]
    w = weight[...]
    lane = lax.broadcasted_iota(jnp.int32, (w.shape[0], 2 * r), 1)

    def outer(m):
        x = bufs[bits - 1][m]
        double = jnp.where(lane < r, pltpu.roll(x, r, 1), x)
        right = jnp.concatenate([double] * (seqs // 2), axis=1) * w
        value = lax.dot_general(
            x, right, TN, preferred_element_type=jnp.float32, precision=lax.Precision.HIGHEST
        )[:r]
        low = m * r
        while low < (m + 1) * r:
            owner, inside = divmod(low, rows_own)
            count = min(rows_own - inside, (m + 1) * r - low)
            index = tuple((owner >> b) & 1 for b in reversed(range(bits)))
            begin = low - m * r
            send2[index + (slice(inside, inside + count), slice(None))] = value[begin : begin + count]
            low += count

    for m in range(MODULES):
        take(m, 0)
    for d in range(MODULES + bits - 2):
        for j in range(bits - 1, 0, -1):
            m = d - (j - 1)
            if 0 <= m < MODULES:
                take(m, j)
                if j == bits - 1:
                    outer(m)

    for j in range(bits):
        source = send2 if j == 0 else bufs2[j - 1]
        copy = send(source, (), bufs2[j], (), j, s2.at[j], r2.at[j])
        copy.start()
        copy.wait()
        bufs2[j][...] = bufs2[j][...] + part(source, (), j, mine[j])[...]

    grads = bufs2[bits - 1][...].astype(jnp.bfloat16)
    exact = grads.astype(jnp.float32)
    features = queries.shape[1]
    tiles = pl.cdiv(features, 2 * r)
    lane_row = lax.broadcasted_iota(jnp.int32, (rows_own, tiles * 2 * r), 1) // r
    own_row = lax.broadcasted_iota(jnp.int32, (rows_own, tiles * 2 * r), 0)
    half = lax.broadcasted_iota(jnp.int32, (rows_own, 2 * r), 1) < r
    flat = []
    for s in range(seqs):
        pair = exact[:, (s // 2) * 2 * r : (s // 2 + 1) * 2 * r]
        other = pltpu.roll(pair, r, 1)
        double = jnp.where(half, pair, other) if s % 2 == 0 else jnp.where(half, other, pair)
        spread = jnp.concatenate([double] * tiles, axis=1)
        flat.append(jnp.sum(jnp.where(lane_row == own_row, spread, 0.0), axis=0, keepdims=True))
    flat = jnp.concatenate(flat + [jnp.zeros_like(flat[0])] * (8 - seqs), axis=0)
    flat = flat[:, :features].astype(jnp.bfloat16)
    grads_out[...] = flat[:seqs]
    score[0] = mm(flat, queries[...])

    for j in range(bits):
        copy = pltpu.make_async_remote_copy(
            src_ref=score.at[j],
            dst_ref=score_in.at[j],
            send_sem=s3.at[j],
            recv_sem=r3.at[j],
            device_id={"tensor": partner[j]},
            device_id_type=MESH,
        )
        copy.start()
        copy.wait()
        score[j + 1] = score[j] + score_in[j]
    total = score[bits]
    result = jnp.zeros((seqs, q_own), jnp.float32)
    for d in range(n):
        result = jnp.where(me == d, total[:seqs, d * q_own : (d + 1) * q_own], result)
    scores_out[...] = result


def reduce_and_score(n, proj, weight, queries, seqs):
    bits = n.bit_length() - 1
    modules, live, lanes = proj.shape
    r = lanes // 2
    rows = live // n
    rows_own = modules * r // n
    q_own = queries.shape[0] // n
    proj = proj.reshape((modules,) + (2,) * bits + (rows, lanes))
    f32 = jnp.float32
    dma = pltpu.SemaphoreType.DMA
    vmem = pl.BlockSpec(memory_space=pltpu.VMEM)
    return pl.pallas_call(
        functools.partial(reduce_kernel, n, bits, q_own, seqs),
        in_specs=[pl.BlockSpec(memory_space=pl.ANY), vmem, vmem],
        out_specs=[vmem, vmem],
        out_shape=[
            jax.ShapeDtypeStruct((seqs, rows_own * r), jnp.bfloat16),
            jax.ShapeDtypeStruct((seqs, q_own), f32),
        ],
        scratch_shapes=[pltpu.VMEM((modules,) + (2,) * (bits - 1) + (rows, lanes), f32)]
        + [pltpu.VMEM((modules,) + (2,) * (bits - 1 - j) + (rows, lanes), f32) for j in range(bits)]
        + [pltpu.VMEM((2,) * bits + (rows_own, seqs * r), f32)]
        + [pltpu.VMEM((2,) * (bits - 1 - j) + (rows_own, seqs * r), f32) for j in range(bits)]
        + [
            pltpu.VMEM((bits + 1, 8, queries.shape[0]), f32),
            pltpu.VMEM((bits, 8, queries.shape[0]), f32),
            dma((modules,)),
            dma((modules, bits)),
            dma((modules, bits)),
            dma((bits,)),
            dma((bits,)),
            dma((bits,)),
            dma((bits,)),
        ],
        compiler_params=pltpu.CompilerParams(
            collective_id=0, has_side_effects=True, vmem_limit_bytes=60 * 2**20
        ),
    )(proj, weight, queries)


def body(n, *arrays):
    queries, lengths = arrays[18], arrays[19]
    seqs, maxlen = arrays[0].shape[:2]
    r = arrays[10].shape[1]
    live = seqs * maxlen // 2
    proj = project(arrays[:18], lengths, live)
    rows = live // n
    ids = lax.axis_index("tensor") * rows + jnp.arange(rows, dtype=jnp.int32)
    ends = jnp.cumsum(lengths)
    inside = (ids[:, None] >= (ends - lengths)[None, :]) & (ids[:, None] < ends[None, :])
    weight = inside.astype(jnp.float32) / lengths.astype(jnp.float32)[None, :]
    weight = jnp.repeat(weight, r, axis=1)
    return reduce_and_score(n, proj, weight, queries, seqs)


def solution(mesh):
    features = P("dom", None, "tensor")
    pair = P("dom", None, None, "tensor")
    one, many = P("tensor", None), P(None, "tensor", None)
    return jax.shard_map(
        functools.partial(body, mesh.shape["tensor"]),
        mesh=mesh,
        in_specs=(
            features, features, pair, features, features, features, pair, features, features,
            many, one, many, one, one, many, one, many, one, P(None, "tensor"), P("dom"),
        ),
        out_specs=(P("dom", "tensor"), P("dom", "tensor")),
        check_vma=False,
    )
```

time: 414 us -> 94.2 us (0.23)
  waiting for transfers between devices: 299 us -> 0 us
  Pallas kernels: 0 us -> 85 us
  local copies, waits for them, and re-layouts: 56.4 us -> 4.13 us
  matrix products: 44.3 us -> 0 us
  between operations: 13.9 us -> 1.35 us
    unnamed x5 -> x0, waiting for transfers between devices: 205 us -> none
    reduce_scatter x1 -> x0, waiting for transfers between devices: 94.3 us -> none  [body(): summed = lax.psum_scatter(joined, 'tensor', scatter_dimension=0, tiled=True)]
    pallas_call x0 -> x2, Pallas kernels: none -> 85 us  [the longest x1 68.8 us: reduce_and_score(): pl.pallas_call(functools.partial(reduce_kernel, n, bits, q_own, seqs), in...]
    dot_general x15 -> x0, matrix products: 43.3 us -> none  [the longest x7 21 us: project_pair(): jnp.dot(gradients.reshape(row_total, -1), factor_out, preferred_element_t...]
    unnamed x39 -> x2, local copies, waits for them, and re-layouts: 31.8 us -> 2.58 us
    slice x5 -> x1, local copies, waits for them, and re-layouts: 24.7 us -> 0.58 us  [project(): at = jnp.minimum(ids, ends[-1] - 1)]
  transfers between devices with their start and end apart: 3 -> 0, of which waited for: 3 -> 0; matrix products, arithmetic and copies ran while one was open for 0% -> 0% of each run, Pallas kernels for 0% -> 0%
where the time goes in v1:
time: 94.2 us; the launch traced here: 93.7 us
  Pallas kernels  85 us (90%)
  local copies, waits for them, and re-layouts  4.13 us (4%)
  other arithmetic  3.26 us (3%)
  between operations  1.35 us (1%)
    pallas_call x1, Pallas kernels, reduce_and_score(): pl.pallas_call(functools.partial(reduce_kernel, n, bits, q_own, seqs), in...  68.8 us
    pallas_call x1, Pallas kernels, project(): pl.pallas_call(functools.partial(project_kernel, live_rows), grid_spec=pl...  16.2 us
    unnamed x2, local copies, waits for them, and re-layouts  2.58 us

profile of v1, /device:TPU:0, one launch (start us, length us, event | category | flops | bytes accessed | tf_op | source)
XLA Modules:
  0.0 93.7 jit_solution(14660599542330381547)
XLA Ops:
  0.6 0.8 reduce-window.14
  1.5 0.7 fusion
  2.2 0.2 reduce-window.13
  2.4 0.6 slice.5
  3.6 0.6 compare_convert_fusion
  4.3 0.1 convert_reduce_fusion
  4.4 0.1 convert_divide_fusion
  4.5 0.1 select_reduce_fusion.1
  4.6 0.6 pad_add_fusion.table
  5.2 0.1 copy.22
  5.3 0.1 broadcast_in_dim.35
  5.4 0.8 reshape.96.weight
  6.1 16.2 %shard_map.203 = f32[7,1024,128]{2,1,0:T(8,128)} custom-call(s32[4,10]{1,0:T(4,128)} %pad_add_fusion.table, bf16[4,512,512]{2,1,0:T(8,128)(2,1)} %attn_input.1, bf16[4,512,512]{2,1,0:T(8,128)(2,1)} %grad_query.1, bf16[4,2,64,512]{3,2,1,0:T(8,128)(2,1)} %bitcast.24, bf16[4,512,512]{2,1,0:T(8,128)(2,1)} %attn_mixed.1, bf16[4,512,512]{2,1,0:T(8,128)(2,1)} %grad_attn.1, ...), custom_call_target="tpu_custom_call" | custom-call | tf_op jit(solution)/shard_map/pallas_call | solution.py:142
  22.3 68.8 %shard_map.204 = (bf16[4,1792]{1,0:T(4,128)(2,1)}, f32[4,16]{1,0:T(4,128)}) custom-call(f32[7,2,2,2,2,64,128]{6,5,4,3,2,1,0:T(8,128)} %bitcast.23, f32[64,256]{1,0:T(8,128)} %reshape.96.weight, bf16[256,1792]{1,0:T(8,128)(2,1)} %queries.1), custom_call_target="tpu_custom_call" | custom-call | tf_op jit(solution)/shard_map/pallas_call | solution.py:307
  91.2 1.3 %copy.25 = bf16[4,1792]{1,0:T(4,128)(2,1)} copy(bf16[4,1792]{1,0:T(4,128)(2,1)} %get-tuple-element.11) | data formatting | bytes 28672
  92.5 1.3 %copy.26 = f32[4,16]{1,0:T(4,128)} copy(f32[4,16]{1,0:T(4,128)} %get-tuple-element.12) | data formatting | bytes 512
  (4 shorter events, 0.0 us)

commit v2 on v1

--- a/solution.py
+++ b/solution.py
@@ -107,17 +107,20 @@
     seqs, maxlen = attn_input.shape[:2]
     r = in_mixed.shape[1]
     steps = maxlen // BLOCK + (live_rows - maxlen + (seqs - 1) * (BLOCK - 1)) // BLOCK
-    counts = (lengths + BLOCK - 1) // BLOCK
-    ends = jnp.cumsum(counts)
-    starts = jnp.cumsum(lengths) - lengths
     ids = jnp.arange(steps, dtype=jnp.int32)
-    at = jnp.minimum(ids, ends[-1] - 1)
-    seq = jnp.sum((at[:, None] >= ends[None, :]).astype(jnp.int32), axis=1)
-    pick = seq[:, None] == jnp.arange(seqs, dtype=jnp.int32)[None, :]
-    first = jnp.sum(jnp.where(pick, (ends - counts)[None, :], 0), axis=1)
-    begin = jnp.sum(jnp.where(pick, starts[None, :], 0), axis=1)
-    block = at - first
-    table = jnp.stack([seq, block, begin + block * BLOCK, (ids < ends[-1]).astype(jnp.int32)])
+    sizes = [lengths[s] for s in range(seqs)]
+    counts = [(size + BLOCK - 1) // BLOCK for size in sizes]
+    total = sum(counts)
+    at = jnp.minimum(ids, total - 1)
+    seq, block, start = jnp.zeros_like(ids), at, jnp.zeros_like(ids)
+    end = 0
+    for size, count in zip(sizes[:-1], counts[:-1]):
+        end = end + count
+        past = at >= end
+        seq = seq + past.astype(jnp.int32)
+        block = block - jnp.where(past, count, 0)
+        start = start + jnp.where(past, size, 0)
+    table = jnp.stack([seq, block, start + block * BLOCK, (ids < total).astype(jnp.int32)])
 
     grad_kv = jnp.transpose(grad_kv, (0, 2, 3, 1))
     tr = lambda x: jnp.swapaxes(x, -1, -2)
@@ -166,7 +169,7 @@
     )(table, *data, *factors)
 
 
-def reduce_kernel(n, bits, q_own, seqs, proj, weight, queries, grads_out, scores_out, *scratch):
+def reduce_kernel(n, bits, q_own, seqs, lengths, proj, queries, grads_out, scores_out, *scratch):
     kept = scratch[0]
     bufs = scratch[1 : 1 + bits]
     send2 = scratch[1 + bits]
@@ -176,33 +179,45 @@
     kept_sem, s1, r1, s2, r2, s3, r3 = scratch[4 + 2 * bits :]
     me = lax.axis_index("tensor")
     mine = [lax.rem(me // (1 << j), 2) for j in range(bits)]
-    partner = [me + (1 - 2 * mine[j]) * (1 << j) for j in range(bits)]
     r = proj.shape[-1] // 2
 
+    def peer(mask):
+        return me + sum((1 - 2 * mine[b]) * (1 << b) for b in range(bits) if mask >> b & 1)
+
+    groups = [[1 << b, 2 << b, 3 << b] if b + 1 < bits else [1 << b] for b in range(0, bits, 2)]
+    partners = [mask for group in groups for mask in group]
+    straight = list(range(bits))
+    swapped = [0, 2, 1] + straight[3:] if bits > 3 else straight
+    orders = [swapped if m in (1, 4) else straight for m in range(MODULES)]
+    halves = [straight, swapped]
+
     barrier = pltpu.get_barrier_semaphore()
-    for j in range(bits):
-        pl.semaphore_signal(barrier, inc=1, device_id={"tensor": partner[j]}, device_id_type=MESH)
-    pl.semaphore_wait(barrier, bits)
-
-    def part(ref, lead, j, which):
-        return ref.at[lead + (slice(None),) * (bits - 1 - j) + (which,)]
-
-    def send(ref, lead, into, into_lead, j, ss, rs):
+    for mask in partners:
+        pl.semaphore_signal(barrier, inc=1, device_id={"tensor": peer(mask)}, device_id_type=MESH)
+    pl.semaphore_wait(barrier, len(partners))
+
+    def part(ref, lead, order, j, other):
+        bit = order[j]
+        ahead = sum(b > bit for b in order[j:])
+        which = 1 - mine[bit] if other else mine[bit]
+        return ref.at[lead + (slice(None),) * ahead + (which,)]
+
+    def send(ref, lead, into, order, j, ss, rs):
         return pltpu.make_async_remote_copy(
-            src_ref=part(ref, lead, j, 1 - mine[j]),
-            dst_ref=into.at[into_lead] if into_lead else into,
+            src_ref=part(ref, lead, order, j, True),
+            dst_ref=into.at[lead],
             send_sem=ss,
             recv_sem=rs,
-            device_id={"tensor": partner[j]},
+            device_id={"tensor": peer(1 << order[j])},
             device_id_type=MESH,
         )
 
     def copy1(m, j):
         source = proj if j == 0 else bufs[j - 1]
-        return send(source, (m,), bufs[j], (m,), j, s1.at[m, j], r1.at[m, j])
+        return send(source, (m,), bufs[j], orders[m], j, s1.at[m, j], r1.at[m, j])
 
     def keep(m):
-        return pltpu.make_async_copy(part(proj, (m,), 0, mine[0]), kept.at[m], kept_sem.at[m])
+        return pltpu.make_async_copy(part(proj, (m,), orders[m], 0, False), kept.at[m], kept_sem.at[m])
 
     for m in range(MODULES):
         copy1(m, 0).start()
@@ -214,13 +229,27 @@
             keep(m).wait()
             bufs[0][m] = bufs[0][m] + kept[m]
         else:
-            bufs[j][m] = bufs[j][m] + part(bufs[j - 1], (m,), j, mine[j])[...]
+            bufs[j][m] = bufs[j][m] + part(bufs[j - 1], (m,), orders[m], j, False)[...]
         if j + 1 < bits:
             copy1(m, j + 1).start()
 
     rows_own = send2.shape[-2]
-    w = weight[...]
-    lane = lax.broadcasted_iota(jnp.int32, (w.shape[0], 2 * r), 1)
+    rows = proj.shape[-2]
+    lane = lax.broadcasted_iota(jnp.int32, (rows, 2 * r), 1)
+    ids = lax.broadcasted_iota(jnp.int32, (rows, 2 * r), 0) + me * rows
+    sizes = [lengths[s] for s in range(seqs)]
+    weights = []
+    begin = 0
+    for size in sizes:
+        inside = (ids >= begin) & (ids < begin + size)
+        size = jnp.broadcast_to(size, ids.shape).astype(jnp.float32)
+        weights.append(jnp.where(inside, 1.0 / size, 0.0))
+        begin = begin + sizes[len(weights) - 1]
+    w = jnp.concatenate(
+        [jnp.where(lane < r, weights[s], weights[s + 1]) for s in range(0, seqs, 2)], axis=1
+    )
+
+    half2 = send2.shape[-1]
 
     def outer(m):
         x = bufs[bits - 1][m]
@@ -235,7 +264,10 @@
             count = min(rows_own - inside, (m + 1) * r - low)
             index = tuple((owner >> b) & 1 for b in reversed(range(bits)))
             begin = low - m * r
-            send2[index + (slice(inside, inside + count), slice(None))] = value[begin : begin + count]
+            for h in range(2):
+                send2[(h,) + index + (slice(inside, inside + count), slice(None))] = value[
+                    begin : begin + count, h * half2 : (h + 1) * half2
+                ]
             low += count
 
     for m in range(MODULES):
@@ -248,14 +280,21 @@
                 if j == bits - 1:
                     outer(m)
 
+    def copy2(h, j):
+        source = send2 if j == 0 else bufs2[j - 1]
+        return send(source, (h,), bufs2[j], halves[h], j, s2.at[h, j], r2.at[h, j])
+
+    for h in range(2):
+        copy2(h, 0).start()
     for j in range(bits):
-        source = send2 if j == 0 else bufs2[j - 1]
-        copy = send(source, (), bufs2[j], (), j, s2.at[j], r2.at[j])
-        copy.start()
-        copy.wait()
-        bufs2[j][...] = bufs2[j][...] + part(source, (), j, mine[j])[...]
-
-    grads = bufs2[bits - 1][...].astype(jnp.bfloat16)
+        for h in range(2):
+            copy2(h, j).wait()
+            source = send2 if j == 0 else bufs2[j - 1]
+            bufs2[j][h] = bufs2[j][h] + part(source, (h,), halves[h], j, False)[...]
+            if j + 1 < bits:
+                copy2(h, j + 1).start()
+
+    grads = jnp.concatenate([bufs2[bits - 1][h] for h in range(2)], axis=1).astype(jnp.bfloat16)
     exact = grads.astype(jnp.float32)
     features = queries.shape[1]
     tiles = pl.cdiv(features, 2 * r)
@@ -274,26 +313,35 @@
     grads_out[...] = flat[:seqs]
     score[0] = mm(flat, queries[...])
 
-    for j in range(bits):
-        copy = pltpu.make_async_remote_copy(
-            src_ref=score.at[j],
-            dst_ref=score_in.at[j],
-            send_sem=s3.at[j],
-            recv_sem=r3.at[j],
-            device_id={"tensor": partner[j]},
-            device_id_type=MESH,
-        )
-        copy.start()
-        copy.wait()
-        score[j + 1] = score[j] + score_in[j]
-    total = score[bits]
+    at = 0
+    for g, group in enumerate(groups):
+        copies = [
+            pltpu.make_async_remote_copy(
+                src_ref=score.at[g],
+                dst_ref=score_in.at[at + k],
+                send_sem=s3.at[at + k],
+                recv_sem=r3.at[at + k],
+                device_id={"tensor": peer(mask)},
+                device_id_type=MESH,
+            )
+            for k, mask in enumerate(group)
+        ]
+        for copy in copies:
+            copy.start()
+        total = score[g]
+        for k, copy in enumerate(copies):
+            copy.wait()
+            total = total + score_in[at + k]
+        score[g + 1] = total
+        at += len(group)
+    total = score[len(groups)]
     result = jnp.zeros((seqs, q_own), jnp.float32)
     for d in range(n):
         result = jnp.where(me == d, total[:seqs, d * q_own : (d + 1) * q_own], result)
     scores_out[...] = result
 
 
-def reduce_and_score(n, proj, weight, queries, seqs):
+def reduce_and_score(n, proj, lengths, queries, seqs):
     bits = n.bit_length() - 1
     modules, live, lanes = proj.shape
     r = lanes // 2
@@ -306,7 +354,7 @@
     vmem = pl.BlockSpec(memory_space=pltpu.VMEM)
     return pl.pallas_call(
         functools.partial(reduce_kernel, n, bits, q_own, seqs),
-        in_specs=[pl.BlockSpec(memory_space=pl.ANY), vmem, vmem],
+        in_specs=[pl.BlockSpec(memory_space=pltpu.SMEM), pl.BlockSpec(memory_space=pl.ANY), vmem],
         out_specs=[vmem, vmem],
         out_shape=[
             jax.ShapeDtypeStruct((seqs, rows_own * r), jnp.bfloat16),
@@ -314,38 +362,31 @@
         ],
         scratch_shapes=[pltpu.VMEM((modules,) + (2,) * (bits - 1) + (rows, lanes), f32)]
         + [pltpu.VMEM((modules,) + (2,) * (bits - 1 - j) + (rows, lanes), f32) for j in range(bits)]
-        + [pltpu.VMEM((2,) * bits + (rows_own, seqs * r), f32)]
-        + [pltpu.VMEM((2,) * (bits - 1 - j) + (rows_own, seqs * r), f32) for j in range(bits)]
+        + [pltpu.VMEM((2,) * (bits + 1) + (rows_own, seqs * r // 2), f32)]
+        + [pltpu.VMEM((2,) * (bits - j) + (rows_own, seqs * r // 2), f32) for j in range(bits)]
         + [
             pltpu.VMEM((bits + 1, 8, queries.shape[0]), f32),
-            pltpu.VMEM((bits, 8, queries.shape[0]), f32),
+            pltpu.VMEM((3 * bits, 8, queries.shape[0]), f32),
             dma((modules,)),
             dma((modules, bits)),
             dma((modules, bits)),
-            dma((bits,)),
-            dma((bits,)),
-            dma((bits,)),
-            dma((bits,)),
+            dma((2, bits)),
+            dma((2, bits)),
+            dma((3 * bits,)),
+            dma((3 * bits,)),
         ],
         compiler_params=pltpu.CompilerParams(
             collective_id=0, has_side_effects=True, vmem_limit_bytes=60 * 2**20
         ),
-    )(proj, weight, queries)
+    )(lengths, proj, queries)
 
 
 def body(n, *arrays):
     queries, lengths = arrays[18], arrays[19]
     seqs, maxlen = arrays[0].shape[:2]
-    r = arrays[10].shape[1]
     live = seqs * maxlen // 2
     proj = project(arrays[:18], lengths, live)
-    rows = live // n
-    ids = lax.axis_index("tensor") * rows + jnp.arange(rows, dtype=jnp.int32)
-    ends = jnp.cumsum(lengths)
-    inside = (ids[:, None] >= (ends - lengths)[None, :]) & (ids[:, None] < ends[None, :])
-    weight = inside.astype(jnp.float32) / lengths.astype(jnp.float32)[None, :]
-    weight = jnp.repeat(weight, r, axis=1)
-    return reduce_and_score(n, proj, weight, queries, seqs)
+    return reduce_and_score(n, proj, lengths, queries, seqs)
 
 
 def solution(mesh):

time: 94.2 us -> 96.7 us (1.027)
  between operations: 1.35 us -> 3.28 us
  Pallas kernels: 85 us -> 86.4 us
    add x2 -> x1, other arithmetic: 0.01 us -> 1.89 us  [project(): start + block * BLOCK]
    pallas_call x1, Pallas kernels: 68.8 us -> 70.2 us  [reduce_and_score(): pl.pallas_call(functools.partial(reduce_kernel, n, bits, q_own, seqs), in...]
    convert_element_type x2 -> x1, other arithmetic: 1.39 us -> 0.01 us  [project(): (ids < total).astype(jnp.int32)]
    another operation x3 -> x1, other arithmetic: 1.6 us -> 0.59 us  [project(): jnp.stack([seq, block, start + block * BLOCK, (ids < total).astype(jnp.in...]
where the time goes in v2:
time: 96.7 us; the launch traced here: 96.2 us
  Pallas kernels  86.4 us (89%)
  local copies, waits for them, and re-layouts  4.02 us (4%)
  between operations  3.28 us (3%)
  other arithmetic  2.49 us (3%)
    pallas_call x1, Pallas kernels, reduce_and_score(): pl.pallas_call(functools.partial(reduce_kernel, n, bits, q_own, seqs), in...  70.2 us
    pallas_call x1, Pallas kernels, project(): pl.pallas_call(functools.partial(project_kernel, live_rows), grid_spec=pl...  16.2 us
    unnamed x2, local copies, waits for them, and re-layouts  2.57 us

profile of v2, /device:TPU:0, one launch (start us, length us, event | category | flops | bytes accessed | tf_op | source)
XLA Modules:
  0.0 96.2 jit_solution(9255701802474615237)
XLA Ops:
  0.6 1.5 %fusion.3 = (s32[1]{0:T(128)}, s32[1]{0:T(128)}, s32[1]{0:T(128)}, s32[1]{0:T(128)}) fusion(s32[4]{0:T(128)} %lengths.1), kind=kLoop, calls=%fused_computation.9 | loop fusion | bytes 32 | tf_op jit(solution)/shard_map/slice | solution.py:111
  4.7 1.9 %multiply_add_fusion = (s32[1,10]{1,0:T(1,128)S(1)}, s32[1,10]{1,0:T(1,128)S(1)}, s32[1,10]{1,0:T(1,128)S(1)}) fusion(s32[]{:T(128)} %bitcast.2, s32[]{:T(128)} %bitcast.1, s32[]{:T(128)} %bitcast, s32[]{:T(128)S(6)} %select_n.87, s32[]{:T(128)S(6)} %sub.81, s32[]{:T(128)S(6)} %add.83, s32[]{:T(128)S(6)} %add.84, s32[]{:T(128)S(6)} %select_n.89, s32[]{:T(128)S(6)} %select_n.88), kind=kLoop, calls=%fused_computation.2 | loop fusion | flops 220 | bytes 156 | tf_op jit(solution)/shard_map/add | solution.py:123
  6.6 0.6 pad_add_fusion.table
  7.2 16.2 %shard_map.203 = f32[7,1024,128]{2,1,0:T(8,128)} custom-call(s32[4,10]{1,0:T(4,128)} %pad_add_fusion.table, bf16[4,512,512]{2,1,0:T(8,128)(2,1)} %attn_input.1, bf16[4,512,512]{2,1,0:T(8,128)(2,1)} %grad_query.1, bf16[4,2,64,512]{3,2,1,0:T(8,128)(2,1)} %bitcast.15, bf16[4,512,512]{2,1,0:T(8,128)(2,1)} %attn_mixed.1, bf16[4,512,512]{2,1,0:T(8,128)(2,1)} %grad_attn.1, ...), custom_call_target="tpu_custom_call" | custom-call | tf_op jit(solution)/shard_map/pallas_call | solution.py:145
  23.4 70.2 %shard_map.204 = (bf16[4,1792]{1,0:T(4,128)(2,1)}, f32[4,16]{1,0:T(4,128)}) custom-call(s32[4]{0:T(128)} %lengths.1, f32[7,2,2,2,2,64,128]{6,5,4,3,2,1,0:T(8,128)} %bitcast.14, bf16[256,1792]{1,0:T(8,128)(2,1)} %queries.1), custom_call_target="tpu_custom_call" | custom-call | tf_op jit(solution)/shard_map/pallas_call | solution.py:355
  93.6 1.3 %copy.24 = bf16[4,1792]{1,0:T(4,128)(2,1)} copy(bf16[4,1792]{1,0:T(4,128)(2,1)} %get-tuple-element.11) | data formatting | bytes 28672
  94.9 1.3 %copy.25 = f32[4,16]{1,0:T(4,128)} copy(f32[4,16]{1,0:T(4,128)} %get-tuple-element.12) | data formatting | bytes 512
  (1 shorter events, 0.0 us)
